TPU v7x, 128 devices: a whole 4x4x4 slice. The times are simulated.
128 devices in a mesh: dp: 16 (over x, y), mp: 8 (over z, core).
Axes of the slice: x: 4, y: 4, z: 4, core: 2. Of those that a mesh axis runs over, the one named last changes fastest.
Arguments:
- tokens: bfloat16 [12288, 3072], P('dp', 'mp'), may hold values from -50 to 50
- target: bfloat16 [12288, 12288], P('dp', 'mp'), may hold values from -90 to 90
- weight: bfloat16 [3072, 12288], P('dp', 'mp'), may hold values from -0.0234375 to 0.0234375
Outputs:
- update: float32 [3072, 12288], P('dp', 'mp')
All inputs are finite; a program needn't handle non-finite values.
Results may differ from a plain program's by a relative error of at most 0.029.
Values may be sent and summed in bfloat16 or wider, within the bound.
No kernel may reach another device: no remote copies, remote signals or barrier semaphores. Data moves between devices by JAX's collectives and lax.ppermute only.
A program may use at most 128 MiB of HBM per device.

v0:
```python
import math

import jax
import jax.numpy as jnp
from jax import lax
from jax.sharding import PartitionSpec as P


def slope_of(hidden, target):
    values, pullback = jax.vjp(jax.nn.gelu, hidden)
    (deriv,) = pullback(jnp.ones_like(hidden))
    return ((values - target.astype(jnp.float32)) * deriv).astype(jnp.bfloat16)


def per_device(tokens, target, weight):
    whole_x = lax.all_gather(tokens, "mp", axis=1, tiled=True)
    columns = weight.shape[1]
    width = whole_x.shape[1]
    hidden_all = columns * lax.axis_size("mp")

    def add_rows(piece):
        return jnp.dot(whole_x, piece, preferred_element_type=jnp.float32)

    def term_maker(slope):
        return lax.dot_general(
            whole_x, slope, (((0,), (0,)), ((), ())), preferred_element_type=jnp.float32
        )

    hidden = add_rows(lax.all_gather(weight, "dp", axis=0, tiled=True))
    slope = slope_of(hidden, target)
    first = lax.psum_scatter(
        term_maker(slope).astype(jnp.bfloat16), "dp", scatter_dimension=0, tiled=True
    ).astype(jnp.float32)
    total = lax.psum(jnp.sum(first * first), ("dp", "mp"))
    scale = 0.5 * math.sqrt(hidden_all) / jnp.sqrt(total + 1e-06)
    shifted = (weight.astype(jnp.float32) + scale * first).astype(jnp.bfloat16)
    hidden_next = add_rows(lax.all_gather(shifted, "dp", axis=0, tiled=True))
    slope_next = slope_of(hidden_next, target)
    second = lax.psum_scatter(
        term_maker(slope_next).astype(jnp.bfloat16), "dp", scatter_dimension=0, tiled=True
    ).astype(jnp.float32)
    total_next = lax.psum(jnp.sum(second * second), ("dp", "mp"))
    factor = jnp.minimum(1.0, math.sqrt(width * hidden_all) / jnp.sqrt(total_next + 1e-06))
    return second * factor


def solution(mesh):
    return jax.shard_map(
        per_device,
        mesh=mesh,
        in_specs=(P("dp", "mp"), P("dp", "mp"), P("dp", "mp")),
        out_specs=P("dp", "mp"),
        check_vma=False,
    )
```

profile of v0, /device:TPU:0, one launch (start us, length us, event | category | flops | bytes accessed | tf_op | source)
XLA Modules:
  0.0 618.8 jit_solution(7312535873656058279)
XLA Ops:
  6.5 0.0 all-gather.4.cloned.1.call-start
  6.5 0.7 all-gather.4.cloned.1.call-update
  7.3 0.0 all-gather.6.cloned.1.call-start
  7.3 0.7 all-gather.6.cloned.1.call-update
  8.0 0.0 reduce-scatter.7.cloned.1.call-start
  8.1 38.0 %all-gather.4.cloned.1.call-done = bf16[768,3072]{1,0:T(8,128)(2,1)} async-done(((bf16[768,384]{1,0:T(8,128)(2,1)}), bf16[768,3072]{1,0:T(8,128)(2,1)}) %all-gather.4.cloned.1.call-update) | async-done | bytes 4718608 | tf_op jit(solution)/shard_map/all_gather | solution.py:16
  46.0 77.7 %all-gather.6.cloned.1.call-done = bf16[3072,1536]{1,0:T(8,128)(2,1)} async-done(((bf16[192,1536]{1,0:T(8,128)(2,1)}), bf16[3072,1536]{1,0:T(8,128)(2,1)}) %all-gather.6.cloned.1.call-update) | async-done | bytes 9437200 | tf_op jit(solution)/shard_map/all_gather | solution.py:29
  123.7 39.4 %fusion = bf16[3072,1536]{0,1:T(8,128)(2,1)} fusion(bf16[768,3072]{1,0:T(8,128)(2,1)} %all-gather.4.cloned.1.call-done, bf16[768,1536]{1,0:T(8,128)(2,1)} %param.4, bf16[3072,1536]{1,0:T(8,128)(2,1)} %all-gather.6.cloned.1.call-done), kind=kOutput, calls=%fused_computation.2 | convolution fusion | flops 14526185472 | bytes 25952256 | tf_op jit(solution)/shard_map/dot_general | solution.py:25
  163.1 12.7 %copy.15 = bf16[3072,1536]{1,0:T(8,128)(2,1)} copy(bf16[3072,1536]{0,1:T(8,128)(2,1)} %fusion) | data formatting | bytes 18874368
  175.8 0.0 copy-start
  175.8 0.0 copy-start.1
  175.8 0.0 reduce-scatter.7.cloned.1.call-update
  175.9 0.0 all-gather.8.cloned.1.call-start
  175.9 87.2 %reduce-scatter.7.cloned.1.call-done = bf16[192,1536]{1,0:T(8,128)(2,1)} async-done(((bf16[3072,1536]{1,0:T(8,128)(2,1)}), bf16[192,1536]{1,0:T(8,128)(2,1)}) %reduce-scatter.7.cloned.1.call-update) | async-done | bytes 589840 | tf_op jit(solution)/shard_map/reduce_scatter | solution.py:31
  263.1 2.0 fusion.33
  265.1 64.7 %psum.14 = f32[]{:T(128)} all-reduce(f32[]{:T(128)} %fusion.33), channel_id=1, replica_groups=mesh['dp'=16,'mp'=8] {'dp','mp'}, use_global_device_ids=true, to_apply=%region_2.0 | all-reduce | flops 1 | bytes 8 | tf_op jit(solution)/shard_map/psum | solution.py:34
  330.5 0.0 copy-done
  330.5 2.1 fusion.35
  332.6 0.0 all-gather.8.cloned.1.call-update
  332.6 0.0 reduce-scatter.9.cloned.1.call-start
  332.7 71.8 %all-gather.8.cloned.1.call-done = bf16[3072,1536]{1,0:T(8,128)(2,1)} async-done(((bf16[192,1536]{1,0:T(8,128)(2,1)}), bf16[3072,1536]{1,0:T(8,128)(2,1)}) %all-gather.8.cloned.1.call-update) | async-done | bytes 9437200 | tf_op jit(solution)/shard_map/all_gather | solution.py:37
  404.5 0.0 copy-done.1
  404.5 38.8 %fusion.1 = bf16[3072,1536]{0,1:T(8,128)(2,1)} fusion(bf16[768,3072]{1,0:T(8,128)(2,1)} %all-gather.4.cloned.1.call-done, bf16[768,1536]{1,0:T(8,128)(2,1)S(1)} %copy-done.1, bf16[3072,1536]{1,0:T(8,128)(2,1)} %all-gather.8.cloned.1.call-done), kind=kOutput, calls=%fused_computation.3 | convolution fusion | flops 14526185472 | bytes 25952256 | tf_op jit(solution)/shard_map/dot_general | solution.py:25
  443.3 12.7 %copy.17 = bf16[3072,1536]{1,0:T(8,128)(2,1)} copy(bf16[3072,1536]{0,1:T(8,128)(2,1)} %fusion.1) | data formatting | bytes 18874368
  456.0 0.0 reduce-scatter.9.cloned.1.call-update
  456.0 87.2 %reduce-scatter.9.cloned.1.call-done = bf16[192,1536]{1,0:T(8,128)(2,1)} async-done(((bf16[3072,1536]{1,0:T(8,128)(2,1)}), bf16[192,1536]{1,0:T(8,128)(2,1)}) %reduce-scatter.9.cloned.1.call-update) | async-done | bytes 589840
  543.2 1.3 copy.18
  544.5 1.0 fusion.32
  545.5 64.5 %psum.15 = f32[]{:T(128)} all-reduce(f32[]{:T(128)} %fusion.32), channel_id=1, replica_groups=mesh['dp'=16,'mp'=8] {'dp','mp'}, use_global_device_ids=true, to_apply=%region_5.0 | all-reduce | flops 1 | bytes 8 | tf_op jit(solution)/shard_map/psum | solution.py:42
  610.7 0.1 convert_multiply_fusion
  610.8 1.5 copy.13
Async XLA Ops:
  6.5 39.5 %all-gather.4.cloned.1.call-start = ((), (), s32[]{:S(2)}) async-start(), calls=%async_computation.2 | async-start | bytes 5308416 | tf_op jit(solution)/shard_map/all_gather | solution.py:16
  7.3 116.4 %all-gather.6.cloned.1.call-start = ((), (), s32[]{:S(2)}) async-start(), calls=%async_computation.3 | async-start | bytes 10027008 | tf_op jit(solution)/shard_map/all_gather | solution.py:29
  8.0 255.1 %reduce-scatter.7.cloned.1.call-start = ((), (), s32[]{:S(2)}) async-start(), calls=%async_computation.5 | async-start | bytes 10027008 | tf_op jit(solution)/shard_map/reduce_scatter | solution.py:31
  175.8 154.7 %copy-start = (bf16[192,1536]{1,0:T(8,128)(2,1)S(1)}, bf16[192,1536]{1,0:T(8,128)(2,1)}, u32[]{:S(2)}) copy-start(bf16[192,1536]{1,0:T(8,128)(2,1)} %param.5) | copy-start | bytes 1769476
  175.8 228.7 %copy-start.1 = (bf16[768,1536]{1,0:T(8,128)(2,1)S(1)}, bf16[768,1536]{1,0:T(8,128)(2,1)}, u32[]{:S(2)}) copy-start(bf16[768,1536]{1,0:T(8,128)(2,1)} %param.4) | copy-start | bytes 7077892
  175.9 228.6 %all-gather.8.cloned.1.call-start = ((), (), s32[]{:S(2)}) async-start(), calls=%async_computation.4 | async-start | bytes 10027008 | tf_op jit(solution)/shard_map/all_gather | solution.py:37
  332.6 210.6 %reduce-scatter.9.cloned.1.call-start = ((), (), s32[]{:S(2)}) async-start(), calls=%async_computation.6 | async-start | bytes 10027008
Sparse Core Ops, SparseCore 0:
  9.1 36.9 all-gather.3
  48.2 75.4 all-gather.5
  176.0 87.1 reduce-scatter.6
  332.7 71.6 all-gather.7
  456.1 87.0 reduce-scatter.8
where the time goes:
time: 620 us; the launch traced here: 619 us
  waiting for transfers between devices  363 us (59%)
  blocking collectives  129 us (21%)
  matrix products  78.2 us (13%)
  local copies, waits for them, and re-layouts  28.2 us (5%)
  between operations  14.6 us (2%)
    unnamed x6, waiting for transfers between devices  88.6 us
    reduce_scatter x1, waiting for transfers between devices, per_device(): lax.psum_scatter(term_maker(slope).astype(jnp.bfloat16), 'dp', scatter_di...  87.2 us
    dot_general x2, matrix products, term_maker(): lax.dot_general(whole_x, slope, (((0,), (0,)), ((), ())), preferred_eleme...  78.2 us
    all_gather x1, waiting for transfers between devices, per_device(): hidden = add_rows(lax.all_gather(weight, 'dp', axis=0, tiled=True))  77.7 us
    all_gather x1, waiting for transfers between devices, per_device(): hidden_next = add_rows(lax.all_gather(shifted, 'dp', axis=0, tiled=True))  71.8 us
    psum x1, blocking collectives, per_device(): total = lax.psum(jnp.sum(first * first), ('dp', 'mp'))  64.7 us
    psum x1, blocking collectives, per_device(): total_next = lax.psum(jnp.sum(second * second), ('dp', 'mp'))  64.5 us
    all_gather x1, waiting for transfers between devices, per_device(): whole_x = lax.all_gather(tokens, 'mp', axis=1, tiled=True)  38 us
  transfers between devices with their start and end apart: 5, of which 5 were waited for; matrix products, arithmetic and copies ran while one was open for 0% of the time, Pallas kernels for 0%

commit v1 on v0

v1 whole, which is shorter than its diff:
```python
import functools
import math

import jax
import jax.numpy as jnp
from jax import lax
from jax.experimental import pallas as pl
from jax.experimental.pallas import tpu as pltpu
from jax.sharding import Mesh, PartitionSpec as P

BF16, F32 = jnp.bfloat16, jnp.float32
N = 4
TILE = 512


def shift(value, axis, step):
    return lax.ppermute(value, axis, [(i, (i + step) % N) for i in range(N)])


def slope_of(hidden, target):
    root = math.sqrt(2.0 / math.pi)
    square = hidden * hidden
    bend = jnp.tanh(root * hidden * (1.0 + 0.044715 * square))
    half = 0.5 * (1.0 + bend)
    deriv = half + (0.5 * root) * hidden * (1.0 - bend * bend) * (1.0 + (3 * 0.044715) * square)
    return ((hidden * half - target.astype(F32)) * deriv).astype(BF16)


def product(x_ref, w_ref):
    x = jnp.concatenate([x_ref[k] for k in range(x_ref.shape[0])], axis=1)
    return jnp.dot(x, w_ref[...], preferred_element_type=F32)


def first_kernel(x_ref, w_ref, t_ref, h_ref, s_ref):
    hidden = product(x_ref, w_ref)
    h_ref[...] = hidden
    s_ref[...] = slope_of(hidden, t_ref[...])


def second_kernel(scale_ref, x_ref, w_ref, t_ref, h_ref, s_ref):
    hidden = h_ref[...] + scale_ref[0, 0] * product(x_ref, w_ref)
    s_ref[...] = slope_of(hidden, t_ref[...])


def slopes(x, w, t, hidden=None, scale=None):
    blocks, rows, wide = x.shape
    cols = w.shape[1]
    tile = pl.BlockSpec((TILE, cols), lambda i: (i, 0))
    x_spec = pl.BlockSpec((blocks, TILE, wide), lambda i: (0, i, 0))
    w_spec = pl.BlockSpec(w.shape, lambda i: (0, 0))
    s_shape = jax.ShapeDtypeStruct((rows, cols), BF16)
    params = pltpu.CompilerParams(vmem_limit_bytes=48 << 20)
    cost = pl.CostEstimate(flops=2 * rows * cols * blocks * wide, bytes_accessed=x.size * 2, transcendentals=rows * cols)
    if hidden is None:
        return pl.pallas_call(
            first_kernel,
            grid=(rows // TILE,),
            in_specs=[x_spec, w_spec, tile],
            out_specs=[tile, tile],
            out_shape=[jax.ShapeDtypeStruct((rows, cols), F32), s_shape],
            compiler_params=params,
            cost_estimate=cost,
        )(x, w, t)
    return pl.pallas_call(
        second_kernel,
        grid=(rows // TILE,),
        in_specs=[pl.BlockSpec(memory_space=pltpu.SMEM), x_spec, w_spec, tile, tile],
        out_specs=tile,
        out_shape=s_shape,
        compiler_params=params,
        cost_estimate=cost,
    )(scale, x, w, t, hidden)


def term_kernel(which_ref, x_ref, s_ref, o_ref):
    o_ref[...] = lax.dot_general(
        x_ref[0], s_ref[...], (((0,), (0,)), ((), ())), preferred_element_type=F32
    )


def term(x, s, block):
    blocks, rows, wide = x.shape
    cols = s.shape[1]
    return pl.pallas_call(
        term_kernel,
        grid_spec=pltpu.PrefetchScalarGridSpec(
            num_scalar_prefetch=1,
            grid=(2,),
            in_specs=[
                pl.BlockSpec((1, rows, wide), lambda k, which: (2 * which[0] + k, 0, 0)),
                pl.BlockSpec((rows, cols), lambda k, which: (0, 0)),
            ],
            out_specs=pl.BlockSpec((wide, cols), lambda k, which: (k, 0)),
        ),
        out_shape=jax.ShapeDtypeStruct((2 * wide, cols), F32),
        compiler_params=pltpu.CompilerParams(vmem_limit_bytes=48 << 20),
        cost_estimate=pl.CostEstimate(flops=4 * rows * cols * wide, bytes_accessed=rows * wide * 4, transcendentals=0),
    )(jnp.reshape(block, (1,)).astype(jnp.int32), x, s)


def ring_sum(part, me):
    block = lambda step: part(lax.rem(me + step, N))
    far = block(2).astype(BF16)
    half = far.shape[0] // 2
    far_next, far_prev = shift(far[:half], "x", 1), shift(far[half:], "x", -1)
    to_next, to_prev = block(1), block(3)
    next_low = shift(to_next[half:].astype(BF16), "x", 1)
    prev_high = shift(to_prev[:half].astype(BF16), "x", -1)
    next_high = shift((to_next[:half] + far_next.astype(F32)).astype(BF16), "x", 1)
    prev_low = shift((to_prev[half:] + far_prev.astype(F32)).astype(BF16), "x", -1)
    own = block(0)
    high = own[:half] + next_high.astype(F32) + prev_high.astype(F32)
    low = own[half:] + next_low.astype(F32) + prev_low.astype(F32)
    return jnp.concatenate([high, low], axis=0)


def ring_gather(value, axis):
    half = value.shape[0] // 2
    high, low = value[:half], value[half:]
    prev_high, next_low = shift(high, axis, 1), shift(low, axis, -1)
    prev_low, next_high = shift(low, axis, 1), shift(high, axis, -1)
    far_high, far_low = shift(prev_high, axis, 1), shift(next_low, axis, -1)
    join = lambda a, b: jnp.concatenate([a, b], axis=0)
    return jnp.stack([value, join(next_high, next_low), join(far_high, far_low), join(prev_high, prev_low)])


def ring_swap(chunk, axis):
    far = chunk(2)
    half = far.shape[0] // 2
    from_prev, from_next = shift(chunk(1), axis, 1), shift(chunk(3), axis, -1)
    far_high = shift(shift(far[:half], axis, 1), axis, 1)
    far_low = shift(shift(far[half:], axis, -1), axis, -1)
    return jnp.stack([chunk(0), from_next, jnp.concatenate([far_high, far_low], axis=0), from_prev])


def in_order(stacked, me):
    twice = jnp.concatenate([stacked, stacked], axis=0)
    return lax.dynamic_slice_in_dim(twice, lax.rem(N - me, N), N, axis=0)


def total_of(value):
    total = jnp.full((8, 128), jnp.sum(value * value), F32)
    total = total + lax.ppermute(total, "c", [(0, 1), (1, 0)])
    for axis in ("x", "y", "z"):
        total = total + shift(total, axis, 1) + shift(total, axis, -1) + shift(total, axis, 2)
    return total[0, 0]


def per_device(tokens, target, weight):
    ix, iy = lax.axis_index("x"), lax.axis_index("y")
    rows, wide = tokens.shape
    cols = weight.shape[1] // N
    width = wide * 2 * N
    hidden_all = weight.shape[1] * 2 * N

    x = lax.all_gather(tokens, ("z", "c", "y"), axis=0, tiled=True).reshape(2 * N, N * rows, wide)

    def columns(array):
        return lambda k: lax.dynamic_slice_in_dim(array, lax.rem(iy + k, N) * cols, cols, axis=1)

    w_rows = in_order(ring_swap(columns(weight), "y"), iy).reshape(-1, cols)
    w = in_order(ring_gather(w_rows, "x"), ix).reshape(width, cols)
    t = in_order(ring_swap(columns(target), "y"), iy).reshape(N * rows, cols)

    hidden, slope = slopes(x, w, t)
    first = ring_sum(lambda b: term(x, slope, b), ix)
    scale = 0.5 * math.sqrt(hidden_all) / jnp.sqrt(total_of(first) + 1e-06)
    shifts = in_order(ring_gather(first.astype(BF16), "x"), ix).reshape(width, cols)
    slope = slopes(x, shifts, t, hidden, scale.reshape(1, 1))
    second = ring_sum(lambda b: term(x, slope, b), ix)
    total = total_of(second)
    factor = jnp.minimum(1.0, math.sqrt(width * hidden_all) / jnp.sqrt(total + 1e-06))
    held = second.astype(BF16).reshape(N, -1, cols)
    parts = in_order(ring_swap(lambda k: lax.dynamic_index_in_dim(held, lax.rem(iy + k, N), 0, keepdims=False), "y"), iy)
    whole = jnp.concatenate([parts[k] for k in range(N)], axis=1)
    return whole.astype(F32) * factor


def solution(mesh):
    grid = Mesh(mesh.devices.reshape(N, N, N, 2), ("x", "y", "z", "c"))
    spec = P(("x", "y"), ("z", "c"))
    return jax.shard_map(
        per_device, mesh=grid, in_specs=(spec, spec, spec), out_specs=spec, check_vma=False
    )
```

time: 620 us -> 310 us (0.50)
  waiting for transfers between devices: 363 us -> 95.9 us
  blocking collectives: 129 us -> 0 us
  starting transfers between devices: 0.16 us -> 83.2 us
  matrix products: 78.2 us -> 0 us
  Pallas kernels: 0 us -> 67.8 us
    all_gather x3 -> x1, waiting for transfers between devices: 187 us -> 3.75 us  [per_device(): lax.all_gather(tokens, ('z', 'c', 'y'), axis=0, tiled=True)]
    psum x2 -> x0, blocking collectives: 129 us -> none  [the longest x1 64.7 us: per_device(): total = lax.psum(jnp.sum(first * first), ('dp', 'mp'))]
    ppermute x0 -> x62, waiting for transfers between devices: none -> 91.4 us  [the longest x60 89.1 us: shift(): return lax.ppermute(value, axis, [(i, (i + step) % N) for i in range(N)])]
    unnamed x6 -> x1, waiting for transfers between devices: 88.6 us -> 0.71 us
    reduce_scatter x1 -> x0, waiting for transfers between devices: 87.2 us -> none  [per_device(): lax.psum_scatter(term_maker(slope).astype(jnp.bfloat16), 'dp', scatter_di...]
    ppermute x0 -> x62, starting transfers between devices: none -> 83.2 us  [the longest x60 83 us: shift(): return lax.ppermute(value, axis, [(i, (i + step) % N) for i in range(N)])]
    dot_general x2 -> x0, matrix products: 78.2 us -> none  [term_maker(): lax.dot_general(whole_x, slope, (((0,), (0,)), ((), ())), preferred_eleme...]
    pallas_call x0 -> x10, Pallas kernels: none -> 67.8 us  [the longest x8 36.1 us: term(): pl.pallas_call(term_kernel, grid_spec=pltpu.PrefetchScalarGridSpec(num_sc...]
  transfers between devices with their start and end apart: 5 -> 63, of which waited for: 5 -> 29; matrix products, arithmetic and copies ran while one was open for 0% -> 10% of each run, Pallas kernels for 0% -> 9%
where the time goes in v1:
time: 310 us; the launch traced here: 304 us
  waiting for transfers between devices  95.9 us (31%)
  starting transfers between devices  83.2 us (27%)
  Pallas kernels  67.8 us (22%)
  local copies, waits for them, and re-layouts  29.7 us (10%)
  between operations  15.9 us (5%)
  other arithmetic  11.1 us (4%)
    ppermute x60, waiting for transfers between devices, shift(): return lax.ppermute(value, axis, [(i, (i + step) % N) for i in range(N)])  89.1 us
    ppermute x60, starting transfers between devices, shift(): return lax.ppermute(value, axis, [(i, (i + step) % N) for i in range(N)])  83 us
    pallas_call x8, Pallas kernels, term(): pl.pallas_call(term_kernel, grid_spec=pltpu.PrefetchScalarGridSpec(num_sc...  36.1 us
    pallas_call x1, Pallas kernels, slopes(): pl.pallas_call(first_kernel, grid=(rows // TILE,), in_specs=[x_spec, w_sp...  15.9 us
    pallas_call x1, Pallas kernels, slopes(): pl.pallas_call(second_kernel, grid=(rows // TILE,), in_specs=[pl.BlockSpe...  15.8 us
    unnamed x26, local copies, waits for them, and re-layouts  10.3 us
    dynamic_slice x4, local copies, waits for them, and re-layouts, in_order(): return lax.dynamic_slice_in_dim(twice, lax.rem(N - me, N), N, axis=0)  6.53 us
  transfers between devices with their start and end apart: 63, of which 29 were waited for; matrix products, arithmetic and copies ran while one was open for 10% of the time, Pallas kernels for 9%

profile of v1, /device:TPU:0, one launch (start us, length us, event | category | flops | bytes accessed | tf_op | source)
XLA Modules:
  0.0 303.5 jit_solution(11438835648205239745)
XLA Ops:
  7.3 1.7 constant_dynamic-slice_fusion.10
  9.0 3.1 %collective-permute-start = (bf16[192,384]{1,0:T(8,128)(2,1)}, bf16[192,384]{1,0:T(8,128)(2,1)}, u32[]{:S(2)}, u32[]{:S(2)}) collective-permute-start(bf16[192,384]{1,0:T(8,128)(2,1)} %get-tuple-element.39), channel_id=1, source_target_pairs={{0,24},{8,0},{16,8},{24,16},{1,25},{9,1},{17,9},{25,17},{2,26},{10... | collective-permute-start | bytes 442376 | tf_op jit(solution)/shard_map/ppermute | solution.py:17
  14.8 2.6 constant_dynamic-slice_fusion.6
  17.4 3.1 %collective-permute-start.12 = (bf16[768,384]{1,0:T(8,128)(2,1)}, bf16[768,384]{1,0:T(8,128)(2,1)S(1)}, u32[]{:S(2)}, u32[]{:S(2)}) collective-permute-start(bf16[768,384]{1,0:T(8,128)(2,1)} %get-tuple-element.14), channel_id=1, source_target_pairs={{0,24},{8,0},{16,8},{24,16},{1,25},{9,1},{17,9},{25,17},{2,26},{10... | collective-permute-start | bytes 1769480 | tf_op jit(solution)/shard_map/ppermute | solution.py:17
  22.3 1.9 collective-permute-start.2
  25.2 24.5 %collective-permute-done.4 = bf16[96,384]{1,0:T(8,128)(2,1)S(1)} collective-permute-done((bf16[96,384]{1,0:T(8,128)(2,1)}, bf16[96,384]{1,0:T(8,128)(2,1)S(1)}, u32[]{:S(2)}, u32[]{:S(2)}) %collective-permute-start.4) | collective-permute-done | bytes 73760 | tf_op jit(solution)/shard_map/ppermute | solution.py:17
  55.3 2.8 collective-permute-start.7
  61.0 1.8 collective-permute-start.17
  64.1 1.7 collective-permute-done.7
  65.8 2.8 collective-permute-start.16
  72.7 2.5 collective-permute-start.10
  75.1 5.3 %collective-permute-done.16 = bf16[384,384]{1,0:T(8,128)(2,1)S(1)} collective-permute-done((bf16[384,384]{1,0:T(8,128)(2,1)}, bf16[384,384]{1,0:T(8,128)(2,1)S(1)}, u32[]{:S(2)}, u32[]{:S(2)}) %collective-permute-start.16) | collective-permute-done | bytes 294944 | tf_op jit(solution)/shard_map/ppermute | solution.py:17
  82.0 20.4 %collective-permute-done.14 = bf16[384,384]{1,0:T(8,128)(2,1)S(1)} collective-permute-done((bf16[384,384]{1,0:T(8,128)(2,1)}, bf16[384,384]{1,0:T(8,128)(2,1)S(1)}, u32[]{:S(2)}, u32[]{:S(2)}) %collective-permute-start.14) | collective-permute-done | bytes 294944 | tf_op jit(solution)/shard_map/ppermute | solution.py:17
  107.8 3.4 %constant_dynamic-slice_fusion.5 = bf16[4,768,384]{2,1,0:T(8,128)(2,1)} fusion(bf16[8,768,384]{2,1,0:T(8,128)(2,1)} %bitcast_dynamic-update-slice_fusion.1, s32[]{:T(128)S(6)} %select_n.42), kind=kLoop, calls=%fused_computation.92 | loop fusion | bytes 4718596 | tf_op jit(solution)/shard_map/dynamic_slice | solution.py:138
  111.8 1.7 constant_dynamic-slice_fusion.8
  113.5 3.8 %all-gather.2.cloned.1.call-done = bf16[24576,384]{1,0:T(8,128)(2,1)} async-done(((bf16[768,384]{1,0:T(8,128)(2,1)}), bf16[24576,384]{1,0:T(8,128)(2,1)}) %all-gather.2.cloned.1.call-update) | async-done | bytes 18874384 | tf_op jit(solution)/shard_map/all_gather | solution.py:156
  119.0 15.9 %shard_map.37 = (f32[3072,384]{1,0:T(8,128)}, bf16[3072,384]{1,0:T(8,128)(2,1)S(1)}) custom-call(bf16[8,3072,384]{2,1,0:T(8,128)(2,1)} %bitcast.117, bf16[3072,384]{1,0:T(8,128)(2,1)S(1)} %bitcast.116, bf16[3072,384]{1,0:T(8,128)(2,1)} %bitcast.127), custom_call_target="tpu_custom_call" | custom-call | flops 7247757312 | bytes 18874368 | tf_op jit(solution)/shard_map/pallas_call | solution.py:55
  134.9 4.5 %shard_map.40 = f32[768,384]{1,0:T(8,128)S(1)} custom-call(s32[1]{0:T(128)} %bitcast.19.which_ref, bf16[8,3072,384]{2,1,0:T(8,128)(2,1)} %bitcast.118, bf16[3072,384]{1,0:T(8,128)(2,1)S(1)} %get-tuple-element.7.s_ref), custom_call_target="tpu_custom_call" | custom-call | flops 1811939328 | bytes 4718592 | tf_op jit(solution)/shard_map/pallas_call | solution.py:84
  141.1 4.5 %shard_map.41 = f32[768,384]{1,0:T(8,128)S(1)} custom-call(s32[1]{0:T(128)} %bitcast.20.which_ref, bf16[8,3072,384]{2,1,0:T(8,128)(2,1)} %bitcast.119, bf16[3072,384]{1,0:T(8,128)(2,1)S(1)} %get-tuple-element.7.s_ref), custom_call_target="tpu_custom_call" | custom-call | flops 1811939328 | bytes 4718592 | tf_op jit(solution)/shard_map/pallas_call | solution.py:84
  146.4 1.8 collective-permute-start.20
  149.7 4.5 %shard_map.39 = f32[768,384]{1,0:T(8,128)S(1)} custom-call(s32[1]{0:T(128)} %bitcast.18.which_ref, bf16[8,3072,384]{2,1,0:T(8,128)(2,1)} %bitcast.120, bf16[3072,384]{1,0:T(8,128)(2,1)S(1)} %get-tuple-element.7.s_ref), custom_call_target="tpu_custom_call" | custom-call | flops 1811939328 | bytes 4718592 | tf_op jit(solution)/shard_map/pallas_call | solution.py:84
  156.6 5.2 %collective-permute-done.22 = bf16[384,384]{1,0:T(8,128)(2,1)S(1)} collective-permute-done((bf16[384,384]{1,0:T(8,128)(2,1)S(1)}, bf16[384,384]{1,0:T(8,128)(2,1)S(1)}, u32[]{:S(2)}, u32[]{:S(2)}) %collective-permute-start.22) | collective-permute-done | bytes 294944 | tf_op jit(solution)/shard_map/ppermute | solution.py:17
  162.6 3.0 collective-permute-start.23
  165.6 4.5 %shard_map.38 = f32[768,384]{1,0:T(8,128)S(1)} custom-call(s32[1]{0:T(128)} %bitcast.which_ref, bf16[8,3072,384]{2,1,0:T(8,128)(2,1)} %bitcast.121, bf16[3072,384]{1,0:T(8,128)(2,1)S(1)} %get-tuple-element.7.s_ref), custom_call_target="tpu_custom_call" | custom-call | flops 1811939328 | bytes 4718592 | tf_op jit(solution)/shard_map/pallas_call | solution.py:84
  175.1 2.2 collective-permute-start.27
  181.3 2.4 collective-permute-done.25
  187.7 1.8 collective-permute-start.36
  191.1 3.9 %collective-permute-start.33 = (f32[8,128]{1,0:T(8,128)S(1)}, f32[8,128]{1,0:T(8,128)S(1)}, u32[]{:S(2)}, u32[]{:S(2)}) collective-permute-start(f32[8,128]{1,0:T(8,128)S(1)} %add_add_fusion.4), channel_id=1, source_target_pairs={{0,4},{2,6},{4,0},{6,2},{1,5},{3,7},{5,1},{7,3},{8,12},{10,14},{12... | collective-permute-start | bytes 12296 | tf_op jit(solution)/shard_map/ppermute | solution.py:17
  198.8 1.8 collective-permute-start.39
  204.9 3.2 %collective-permute-done.38 = bf16[384,384]{1,0:T(8,128)(2,1)S(1)} collective-permute-done((bf16[384,384]{1,0:T(8,128)(2,1)S(1)}, bf16[384,384]{1,0:T(8,128)(2,1)S(1)}, u32[]{:S(2)}, u32[]{:S(2)}) %collective-permute-start.38) | collective-permute-done | bytes 294944 | tf_op jit(solution)/shard_map/ppermute | solution.py:17
  208.1 3.3 %collective-permute-done.37 = bf16[384,384]{1,0:T(8,128)(2,1)S(1)} collective-permute-done((bf16[384,384]{1,0:T(8,128)(2,1)S(1)}, bf16[384,384]{1,0:T(8,128)(2,1)S(1)}, u32[]{:S(2)}, u32[]{:S(2)}) %collective-permute-start.37) | collective-permute-done | bytes 294944 | tf_op jit(solution)/shard_map/ppermute | solution.py:17
  212.3 15.8 %shard_map.42.s_ref = bf16[3072,384]{1,0:T(8,128)(2,1)S(1)} custom-call(f32[1,1]{1,0:T(1,128)S(6)} %div.6.scale_ref, bf16[8,3072,384]{2,1,0:T(8,128)(2,1)} %bitcast.122, bf16[3072,384]{1,0:T(8,128)(2,1)S(1)} %bitcast.115, bf16[3072,384]{1,0:T(8,128)(2,1)} %bitcast.128, f32[3072,384]{1,0:T(8,128)} %get-tuple-element.8.h_ref), custom_call_target="tpu_custom_call" | custom-call | flops 7247757312 | bytes 18874368 | tf_op jit(solution)/shard_map/pallas_call | solution.py:64
  228.0 4.5 %shard_map.45 = f32[768,384]{1,0:T(8,128)S(1)} custom-call(s32[1]{0:T(128)} %bitcast.19.which_ref, bf16[8,3072,384]{2,1,0:T(8,128)(2,1)} %bitcast.123, bf16[3072,384]{1,0:T(8,128)(2,1)S(1)} %shard_map.42.s_ref), custom_call_target="tpu_custom_call" | custom-call | flops 1811939328 | bytes 4718592 | tf_op jit(solution)/shard_map/pallas_call | solution.py:84
  233.0 3.0 collective-permute-start.44
  236.0 4.5 %shard_map.46 = f32[768,384]{1,0:T(8,128)S(1)} custom-call(s32[1]{0:T(128)} %bitcast.20.which_ref, bf16[8,3072,384]{2,1,0:T(8,128)(2,1)} %bitcast.124, bf16[3072,384]{1,0:T(8,128)(2,1)S(1)} %shard_map.42.s_ref), custom_call_target="tpu_custom_call" | custom-call | flops 1811939328 | bytes 4718592 | tf_op jit(solution)/shard_map/pallas_call | solution.py:84
  240.5 4.5 %shard_map.44 = f32[768,384]{1,0:T(8,128)S(1)} custom-call(s32[1]{0:T(128)} %bitcast.18.which_ref, bf16[8,3072,384]{2,1,0:T(8,128)(2,1)} %bitcast.125, bf16[3072,384]{1,0:T(8,128)(2,1)S(1)} %shard_map.42.s_ref), custom_call_target="tpu_custom_call" | custom-call | flops 1811939328 | bytes 4718592 | tf_op jit(solution)/shard_map/pallas_call | solution.py:84
  245.2 2.1 collective-permute-start.43
  247.6 3.5 %collective-permute-start.45 = (bf16[384,384]{1,0:T(8,128)(2,1)S(1)}, bf16[384,384]{1,0:T(8,128)(2,1)S(1)}, u32[]{:S(2)}, u32[]{:S(2)}) collective-permute-start(bf16[384,384]{1,0:T(8,128)(2,1)S(1)} %fusion.2), channel_id=1, source_target_pairs={{0,96},{32,0},{64,32},{96,64},{1,97},{33,1},{65,33},{97,65},{2,98}... | collective-permute-start | bytes 884744 | tf_op jit(solution)/shard_map/ppermute | solution.py:17
  251.1 4.5 %shard_map.43 = f32[768,384]{1,0:T(8,128)S(1)} custom-call(s32[1]{0:T(128)} %bitcast.which_ref, bf16[8,3072,384]{2,1,0:T(8,128)(2,1)} %bitcast.126, bf16[3072,384]{1,0:T(8,128)(2,1)S(1)} %shard_map.42.s_ref), custom_call_target="tpu_custom_call" | custom-call | flops 1811939328 | bytes 4718592 | tf_op jit(solution)/shard_map/pallas_call | solution.py:84
  261.0 2.6 collective-permute-start.54
  265.2 3.2 %collective-permute-done.53 = f32[8,128]{1,0:T(8,128)S(1)} collective-permute-done((f32[8,128]{1,0:T(8,128)S(1)}, f32[8,128]{1,0:T(8,128)S(1)}, u32[]{:S(2)}, u32[]{:S(2)}) %collective-permute-start.53) | collective-permute-done | bytes 4128 | tf_op jit(solution)/shard_map/ppermute | solution.py:17
  269.1 2.7 collective-permute-start.58
  271.8 1.7 collective-permute-start.57
  273.8 3.0 collective-permute-start.46
  279.9 2.1 collective-permute-start.60
  284.2 2.6 collective-permute-done.59
  290.2 2.3 collective-permute-done.50
  292.5 2.4 collective-permute-done.48
  (182 shorter events, 76.9 us)
Async XLA Ops:
  6.5 110.7 %all-gather.2.cloned.1.call-start = ((), (), s32[]{:S(2)}) async-start(), calls=%async_computation | async-start | bytes 19464192 | tf_op jit(solution)/shard_map/all_gather | solution.py:156
  9.0 13.3 %collective-permute-start = (bf16[192,384]{1,0:T(8,128)(2,1)}, bf16[192,384]{1,0:T(8,128)(2,1)}, u32[]{:S(2)}, u32[]{:S(2)}) collective-permute-start(bf16[192,384]{1,0:T(8,128)(2,1)} %get-tuple-element.39), channel_id=1, source_target_pairs={{0,24},{8,0},{16,8},{24,16},{1,25},{9,1},{17,9},{25,17},{2,26},{10... | collective-permute-start | bytes 442376 | tf_op jit(solution)/shard_map/ppermute | solution.py:17
  12.8 8.6 %collective-permute-start.3 = (bf16[96,384]{1,0:T(8,128)(2,1)}, bf16[96,384]{1,0:T(8,128)(2,1)}, u32[]{:S(2)}, u32[]{:S(2)}) collective-permute-start(bf16[96,384]{1,0:T(8,128)(2,1)} %get-tuple-element.41), channel_id=1, source_target_pairs={{0,24},{8,0},{16,8},{24,16},{1,25},{9,1},{17,9},{25,17},{2,26},{10... | collective-permute-start | bytes 221192 | tf_op jit(solution)/shard_map/ppermute | solution.py:17
  13.5 8.7 %collective-permute-start.1 = (bf16[96,384]{1,0:T(8,128)(2,1)}, bf16[96,384]{1,0:T(8,128)(2,1)}, u32[]{:S(2)}, u32[]{:S(2)}) collective-permute-start(bf16[96,384]{1,0:T(8,128)(2,1)} %get-tuple-element.40), channel_id=1, source_target_pairs={{0,8},{8,16},{16,24},{24,0},{1,9},{9,17},{17,25},{25,1},{2,10},{10... | collective-permute-start | bytes 221192 | tf_op jit(solution)/shard_map/ppermute | solution.py:17
  14.8 35.7 %collective-permute-start.5 = (bf16[192,384]{1,0:T(8,128)(2,1)}, bf16[192,384]{1,0:T(8,128)(2,1)}, u32[]{:S(2)}, u32[]{:S(2)}) collective-permute-start(bf16[192,384]{1,0:T(8,128)(2,1)} %get-tuple-element.38), channel_id=1, source_target_pairs={{0,8},{8,16},{16,24},{24,0},{1,9},{9,17},{17,25},{25,1},{2,10},{10... | collective-permute-start | bytes 442376 | tf_op jit(solution)/shard_map/ppermute | solution.py:17
  17.4 53.1 %collective-permute-start.12 = (bf16[768,384]{1,0:T(8,128)(2,1)}, bf16[768,384]{1,0:T(8,128)(2,1)S(1)}, u32[]{:S(2)}, u32[]{:S(2)}) collective-permute-start(bf16[768,384]{1,0:T(8,128)(2,1)} %get-tuple-element.14), channel_id=1, source_target_pairs={{0,24},{8,0},{16,8},{24,16},{1,25},{9,1},{17,9},{25,17},{2,26},{10... | collective-permute-start | bytes 1769480 | tf_op jit(solution)/shard_map/ppermute | solution.py:17
  21.4 39.5 %collective-permute-start.15 = (bf16[384,384]{1,0:T(8,128)(2,1)}, bf16[384,384]{1,0:T(8,128)(2,1)}, u32[]{:S(2)}, u32[]{:S(2)}) collective-permute-start(bf16[384,384]{1,0:T(8,128)(2,1)} %get-tuple-element.16), channel_id=1, source_target_pairs={{0,24},{8,0},{16,8},{24,16},{1,25},{9,1},{17,9},{25,17},{2,26},{10... | collective-permute-start | bytes 884744 | tf_op jit(solution)/shard_map/ppermute | solution.py:17
  22.2 27.4 %collective-permute-start.4 = (bf16[96,384]{1,0:T(8,128)(2,1)}, bf16[96,384]{1,0:T(8,128)(2,1)S(1)}, u32[]{:S(2)}, u32[]{:S(2)}) collective-permute-start(bf16[96,384]{1,0:T(8,128)(2,1)} %collective-permute-done.3), channel_id=1, source_target_pairs={{0,24},{8,0},{16,8},{24,16},{1,25},{9,1},{17,9},{25,17},{2,26},{10... | collective-permute-start | bytes 221192 | tf_op jit(solution)/shard_map/ppermute | solution.py:17
  22.3 28.1 %collective-permute-start.2 = (bf16[96,384]{1,0:T(8,128)(2,1)}, bf16[96,384]{1,0:T(8,128)(2,1)S(1)}, u32[]{:S(2)}, u32[]{:S(2)}) collective-permute-start(bf16[96,384]{1,0:T(8,128)(2,1)} %collective-permute-done.1), channel_id=1, source_target_pairs={{0,8},{8,16},{16,24},{24,0},{1,9},{9,17},{17,25},{25,1},{2,10},{10... | collective-permute-start | bytes 221192 | tf_op jit(solution)/shard_map/ppermute | solution.py:17
  49.7 13.2 %collective-permute-start.13 = (bf16[384,384]{1,0:T(8,128)(2,1)}, bf16[384,384]{1,0:T(8,128)(2,1)}, u32[]{:S(2)}, u32[]{:S(2)}) collective-permute-start(bf16[384,384]{1,0:T(8,128)(2,1)} %get-tuple-element.15), channel_id=1, source_target_pairs={{0,8},{8,16},{16,24},{24,0},{1,9},{9,17},{17,25},{25,1},{2,10},{10... | collective-permute-start | bytes 884744 | tf_op jit(solution)/shard_map/ppermute | solution.py:17
  55.3 10.5 %collective-permute-start.7 = (bf16[384,384]{1,0:T(8,128)(2,1)}, bf16[384,384]{1,0:T(8,128)(2,1)S(1)}, u32[]{:S(2)}, u32[]{:S(2)}) collective-permute-start(bf16[384,384]{1,0:T(8,128)(2,1)} %bitcast.8), channel_id=1, source_target_pairs={{0,96},{32,0},{64,32},{96,64},{1,97},{33,1},{65,33},{97,65},{2,98}... | collective-permute-start | bytes 884744 | tf_op jit(solution)/shard_map/ppermute | solution.py:17
  58.1 11.0 %collective-permute-start.6 = (bf16[384,384]{1,0:T(8,128)(2,1)}, bf16[384,384]{1,0:T(8,128)(2,1)S(1)}, u32[]{:S(2)}, u32[]{:S(2)}) collective-permute-start(bf16[384,384]{1,0:T(8,128)(2,1)} %bitcast.7), channel_id=1, source_target_pairs={{0,96},{32,0},{64,32},{96,64},{1,97},{33,1},{65,33},{97,65},{2,98}... | collective-permute-start | bytes 884744 | tf_op jit(solution)/shard_map/ppermute | solution.py:17
  61.0 42.4 %collective-permute-start.17 = (bf16[768,384]{1,0:T(8,128)(2,1)S(1)}, bf16[768,384]{1,0:T(8,128)(2,1)S(1)}, u32[]{:S(2)}, u32[]{:S(2)}) collective-permute-start(bf16[768,384]{1,0:T(8,128)(2,1)S(1)} %copy-done.4), channel_id=1, source_target_pairs={{0,8},{8,16},{16,24},{24,0},{1,9},{9,17},{17,25},{25,1},{2,10},{10... | collective-permute-start | bytes 1769480 | tf_op jit(solution)/shard_map/ppermute | solution.py:17
  62.9 9.8 %collective-permute-start.8 = (bf16[384,384]{1,0:T(8,128)(2,1)}, bf16[384,384]{1,0:T(8,128)(2,1)S(1)}, u32[]{:S(2)}, u32[]{:S(2)}) collective-permute-start(bf16[384,384]{1,0:T(8,128)(2,1)} %bitcast.7), channel_id=1, source_target_pairs={{0,32},{32,64},{64,96},{96,0},{1,33},{33,65},{65,97},{97,1},{2,34}... | collective-permute-start | bytes 884744 | tf_op jit(solution)/shard_map/ppermute | solution.py:17
  65.8 14.6 %collective-permute-start.16 = (bf16[384,384]{1,0:T(8,128)(2,1)}, bf16[384,384]{1,0:T(8,128)(2,1)S(1)}, u32[]{:S(2)}, u32[]{:S(2)}) collective-permute-start(bf16[384,384]{1,0:T(8,128)(2,1)} %collective-permute-done.15), channel_id=1, source_target_pairs={{0,24},{8,0},{16,8},{24,16},{1,25},{9,1},{17,9},{25,17},{2,26},{10... | collective-permute-start | bytes 884744 | tf_op jit(solution)/shard_map/ppermute | solution.py:17
  69.0 33.5 %collective-permute-start.14 = (bf16[384,384]{1,0:T(8,128)(2,1)}, bf16[384,384]{1,0:T(8,128)(2,1)S(1)}, u32[]{:S(2)}, u32[]{:S(2)}) collective-permute-start(bf16[384,384]{1,0:T(8,128)(2,1)} %collective-permute-done.13), channel_id=1, source_target_pairs={{0,8},{8,16},{16,24},{24,0},{1,9},{9,17},{17,25},{25,1},{2,10},{10... | collective-permute-start | bytes 884744 | tf_op jit(solution)/shard_map/ppermute | solution.py:17
  70.6 40.7 %collective-permute-start.11 = (bf16[384,384]{1,0:T(8,128)(2,1)}, bf16[384,384]{1,0:T(8,128)(2,1)S(1)}, u32[]{:S(2)}, u32[]{:S(2)}) collective-permute-start(bf16[384,384]{1,0:T(8,128)(2,1)} %bitcast.8), channel_id=1, source_target_pairs={{0,32},{32,64},{64,96},{96,0},{1,33},{33,65},{65,97},{97,1},{2,34}... | collective-permute-start | bytes 884744 | tf_op jit(solution)/shard_map/ppermute | solution.py:17
  72.7 38.5 %collective-permute-start.10 = (bf16[384,384]{1,0:T(8,128)(2,1)S(1)}, bf16[384,384]{1,0:T(8,128)(2,1)S(1)}, u32[]{:S(2)}, u32[]{:S(2)}) collective-permute-start(bf16[384,384]{1,0:T(8,128)(2,1)S(1)} %collective-permute-done.7), channel_id=1, source_target_pairs={{0,96},{32,0},{64,32},{96,64},{1,97},{33,1},{65,33},{97,65},{2,98}... | collective-permute-start | bytes 884744 | tf_op jit(solution)/shard_map/ppermute | solution.py:17
  80.4 30.8 %collective-permute-start.9 = (bf16[384,384]{1,0:T(8,128)(2,1)S(1)}, bf16[384,384]{1,0:T(8,128)(2,1)S(1)}, u32[]{:S(2)}, u32[]{:S(2)}) collective-permute-start(bf16[384,384]{1,0:T(8,128)(2,1)S(1)} %collective-permute-done.8), channel_id=1, source_target_pairs={{0,32},{32,64},{64,96},{96,0},{1,33},{33,65},{65,97},{97,1},{2,34}... | collective-permute-start | bytes 884744 | tf_op jit(solution)/shard_map/ppermute | solution.py:17
  139.6 15.9 %collective-permute-start.18 = (bf16[384,384]{1,0:T(8,128)(2,1)S(1)}, bf16[384,384]{1,0:T(8,128)(2,1)S(1)}, u32[]{:S(2)}, u32[]{:S(2)}) collective-permute-start(bf16[384,384]{1,0:T(8,128)(2,1)S(1)} %get-tuple-element.36), channel_id=1, source_target_pairs={{0,32},{32,64},{64,96},{96,0},{1,33},{33,65},{65,97},{97,1},{2,34}... | collective-permute-start | bytes 884744 | tf_op jit(solution)/shard_map/ppermute | solution.py:17
  146.4 23.7 %collective-permute-start.20 = (bf16[384,384]{1,0:T(8,128)(2,1)}, bf16[384,384]{1,0:T(8,128)(2,1)S(1)}, u32[]{:S(2)}, u32[]{:S(2)}) collective-permute-start(bf16[384,384]{1,0:T(8,128)(2,1)} %slice.197), channel_id=1, source_target_pairs={{0,96},{32,0},{64,32},{96,64},{1,97},{33,1},{65,33},{97,65},{2,98}... | collective-permute-start | bytes 884744 | tf_op jit(solution)/shard_map/ppermute | solution.py:17
  148.1 13.7 %collective-permute-start.22 = (bf16[384,384]{1,0:T(8,128)(2,1)S(1)}, bf16[384,384]{1,0:T(8,128)(2,1)S(1)}, u32[]{:S(2)}, u32[]{:S(2)}) collective-permute-start(bf16[384,384]{1,0:T(8,128)(2,1)S(1)} %get-tuple-element.37), channel_id=1, source_target_pairs={{0,96},{32,0},{64,32},{96,64},{1,97},{33,1},{65,33},{97,65},{2,98}... | collective-permute-start | bytes 884744 | tf_op jit(solution)/shard_map/ppermute | solution.py:17
  155.0 15.1 %collective-permute-start.21 = (bf16[384,384]{1,0:T(8,128)(2,1)}, bf16[384,384]{1,0:T(8,128)(2,1)S(1)}, u32[]{:S(2)}, u32[]{:S(2)}) collective-permute-start(bf16[384,384]{1,0:T(8,128)(2,1)} %slice.196), channel_id=1, source_target_pairs={{0,32},{32,64},{64,96},{96,0},{1,33},{33,65},{65,97},{97,1},{2,34}... | collective-permute-start | bytes 884744 | tf_op jit(solution)/shard_map/ppermute | solution.py:17
  156.3 14.8 %collective-permute-start.19 = (bf16[384,384]{1,0:T(8,128)(2,1)}, bf16[384,384]{1,0:T(8,128)(2,1)S(1)}, u32[]{:S(2)}, u32[]{:S(2)}) collective-permute-start(bf16[384,384]{1,0:T(8,128)(2,1)} %fusion.8), channel_id=1, source_target_pairs={{0,32},{32,64},{64,96},{96,0},{1,33},{33,65},{65,97},{97,1},{2,34}... | collective-permute-start | bytes 884744 | tf_op jit(solution)/shard_map/ppermute | solution.py:17
  162.6 8.8 %collective-permute-start.23 = (bf16[384,384]{1,0:T(8,128)(2,1)}, bf16[384,384]{1,0:T(8,128)(2,1)S(1)}, u32[]{:S(2)}, u32[]{:S(2)}) collective-permute-start(bf16[384,384]{1,0:T(8,128)(2,1)} %fusion.6), channel_id=1, source_target_pairs={{0,96},{32,0},{64,32},{96,64},{1,97},{33,1},{65,33},{97,65},{2,98}... | collective-permute-start | bytes 884744 | tf_op jit(solution)/shard_map/ppermute | solution.py:17
  175.1 5.2 %collective-permute-start.27 = (f32[8,128]{1,0:T(8,128)S(1)}, f32[8,128]{1,0:T(8,128)S(1)}, u32[]{:S(2)}, u32[]{:S(2)}) collective-permute-start(f32[8,128]{1,0:T(8,128)S(1)} %broadcast_add_fusion.1), channel_id=1, source_target_pairs={{0,64},{32,96},{64,0},{96,32},{1,65},{33,97},{65,1},{97,33},{2,66}... | collective-permute-start | bytes 12296 | tf_op jit(solution)/shard_map/ppermute | solution.py:17
  184.4 5.2 %collective-permute-start.30 = (f32[8,128]{1,0:T(8,128)S(1)}, f32[8,128]{1,0:T(8,128)S(1)}, u32[]{:S(2)}, u32[]{:S(2)}) collective-permute-start(f32[8,128]{1,0:T(8,128)S(1)} %add_add_fusion.5), channel_id=1, source_target_pairs={{0,16},{8,24},{16,0},{24,8},{1,17},{9,25},{17,1},{25,9},{2,18},{10... | collective-permute-start | bytes 12296 | tf_op jit(solution)/shard_map/ppermute | solution.py:17
  187.2 13.4 %collective-permute-start.35 = (bf16[384,384]{1,0:T(8,128)(2,1)S(1)}, bf16[384,384]{1,0:T(8,128)(2,1)S(1)}, u32[]{:S(2)}, u32[]{:S(2)}) collective-permute-start(bf16[384,384]{1,0:T(8,128)(2,1)S(1)} %get-tuple-element.35), channel_id=1, source_target_pairs={{0,96},{32,0},{64,32},{96,64},{1,97},{33,1},{65,33},{97,65},{2,98}... | collective-permute-start | bytes 884744 | tf_op jit(solution)/shard_map/ppermute | solution.py:17
  187.7 14.3 %collective-permute-start.36 = (bf16[384,384]{1,0:T(8,128)(2,1)S(1)}, bf16[384,384]{1,0:T(8,128)(2,1)S(1)}, u32[]{:S(2)}, u32[]{:S(2)}) collective-permute-start(bf16[384,384]{1,0:T(8,128)(2,1)S(1)} %get-tuple-element.34), channel_id=1, source_target_pairs={{0,32},{32,64},{64,96},{96,0},{1,33},{33,65},{65,97},{97,1},{2,34}... | collective-permute-start | bytes 884744 | tf_op jit(solution)/shard_map/ppermute | solution.py:17
  191.1 5.5 %collective-permute-start.33 = (f32[8,128]{1,0:T(8,128)S(1)}, f32[8,128]{1,0:T(8,128)S(1)}, u32[]{:S(2)}, u32[]{:S(2)}) collective-permute-start(f32[8,128]{1,0:T(8,128)S(1)} %add_add_fusion.4), channel_id=1, source_target_pairs={{0,4},{2,6},{4,0},{6,2},{1,5},{3,7},{5,1},{7,3},{8,12},{10,14},{12... | collective-permute-start | bytes 12296 | tf_op jit(solution)/shard_map/ppermute | solution.py:17
  195.0 9.8 %collective-permute-start.34 = (bf16[384,384]{1,0:T(8,128)(2,1)S(1)}, bf16[384,384]{1,0:T(8,128)(2,1)S(1)}, u32[]{:S(2)}, u32[]{:S(2)}) collective-permute-start(bf16[384,384]{1,0:T(8,128)(2,1)S(1)} %get-tuple-element.34), channel_id=1, source_target_pairs={{0,96},{32,0},{64,32},{96,64},{1,97},{33,1},{65,33},{97,65},{2,98}... | collective-permute-start | bytes 884744 | tf_op jit(solution)/shard_map/ppermute | solution.py:17
  196.6 6.1 %collective-permute-start.31 = (f32[8,128]{1,0:T(8,128)S(1)}, f32[8,128]{1,0:T(8,128)S(1)}, u32[]{:S(2)}, u32[]{:S(2)}) collective-permute-start(f32[8,128]{1,0:T(8,128)S(1)} %add_add_fusion.4), channel_id=1, source_target_pairs={{0,2},{2,4},{4,6},{6,0},{1,3},{3,5},{5,7},{7,1},{8,10},{10,12},{12... | collective-permute-start | bytes 12296 | tf_op jit(solution)/shard_map/ppermute | solution.py:17
  198.8 12.7 %collective-permute-start.39 = (bf16[384,384]{1,0:T(8,128)(2,1)S(1)}, bf16[384,384]{1,0:T(8,128)(2,1)S(1)}, u32[]{:S(2)}, u32[]{:S(2)}) collective-permute-start(bf16[384,384]{1,0:T(8,128)(2,1)S(1)} %get-tuple-element.35), channel_id=1, source_target_pairs={{0,32},{32,64},{64,96},{96,0},{1,33},{33,65},{65,97},{97,1},{2,34}... | collective-permute-start | bytes 884744 | tf_op jit(solution)/shard_map/ppermute | solution.py:17
  200.7 7.4 %collective-permute-start.38 = (bf16[384,384]{1,0:T(8,128)(2,1)S(1)}, bf16[384,384]{1,0:T(8,128)(2,1)S(1)}, u32[]{:S(2)}, u32[]{:S(2)}) collective-permute-start(bf16[384,384]{1,0:T(8,128)(2,1)S(1)} %collective-permute-done.35), channel_id=1, source_target_pairs={{0,96},{32,0},{64,32},{96,64},{1,97},{33,1},{65,33},{97,65},{2,98}... | collective-permute-start | bytes 884744 | tf_op jit(solution)/shard_map/ppermute | solution.py:17
  202.1 9.3 %collective-permute-start.37 = (bf16[384,384]{1,0:T(8,128)(2,1)S(1)}, bf16[384,384]{1,0:T(8,128)(2,1)S(1)}, u32[]{:S(2)}, u32[]{:S(2)}) collective-permute-start(bf16[384,384]{1,0:T(8,128)(2,1)S(1)} %collective-permute-done.36), channel_id=1, source_target_pairs={{0,32},{32,64},{64,96},{96,0},{1,33},{33,65},{65,97},{97,1},{2,34}... | collective-permute-start | bytes 884744 | tf_op jit(solution)/shard_map/ppermute | solution.py:17
  232.7 14.6 %collective-permute-start.40 = (bf16[384,384]{1,0:T(8,128)(2,1)S(1)}, bf16[384,384]{1,0:T(8,128)(2,1)S(1)}, u32[]{:S(2)}, u32[]{:S(2)}) collective-permute-start(bf16[384,384]{1,0:T(8,128)(2,1)S(1)} %get-tuple-element.32), channel_id=1, source_target_pairs={{0,32},{32,64},{64,96},{96,0},{1,33},{33,65},{65,97},{97,1},{2,34}... | collective-permute-start | bytes 884744 | tf_op jit(solution)/shard_map/ppermute | solution.py:17
  233.0 14.5 %collective-permute-start.44 = (bf16[384,384]{1,0:T(8,128)(2,1)S(1)}, bf16[384,384]{1,0:T(8,128)(2,1)S(1)}, u32[]{:S(2)}, u32[]{:S(2)}) collective-permute-start(bf16[384,384]{1,0:T(8,128)(2,1)S(1)} %get-tuple-element.33), channel_id=1, source_target_pairs={{0,96},{32,0},{64,32},{96,64},{1,97},{33,1},{65,33},{97,65},{2,98}... | collective-permute-start | bytes 884744 | tf_op jit(solution)/shard_map/ppermute | solution.py:17
  245.1 10.5 %collective-permute-start.42 = (bf16[384,384]{1,0:T(8,128)(2,1)S(1)}, bf16[384,384]{1,0:T(8,128)(2,1)S(1)}, u32[]{:S(2)}, u32[]{:S(2)}) collective-permute-start(bf16[384,384]{1,0:T(8,128)(2,1)S(1)} %slice.195), channel_id=1, source_target_pairs={{0,96},{32,0},{64,32},{96,64},{1,97},{33,1},{65,33},{97,65},{2,98}... | collective-permute-start | bytes 884744 | tf_op jit(solution)/shard_map/ppermute | solution.py:17
  245.2 10.4 %collective-permute-start.43 = (bf16[384,384]{1,0:T(8,128)(2,1)S(1)}, bf16[384,384]{1,0:T(8,128)(2,1)S(1)}, u32[]{:S(2)}, u32[]{:S(2)}) collective-permute-start(bf16[384,384]{1,0:T(8,128)(2,1)S(1)} %slice.194), channel_id=1, source_target_pairs={{0,32},{32,64},{64,96},{96,0},{1,33},{33,65},{65,97},{97,1},{2,34}... | collective-permute-start | bytes 884744 | tf_op jit(solution)/shard_map/ppermute | solution.py:17
  247.4 9.0 %collective-permute-start.41 = (bf16[384,384]{1,0:T(8,128)(2,1)S(1)}, bf16[384,384]{1,0:T(8,128)(2,1)S(1)}, u32[]{:S(2)}, u32[]{:S(2)}) collective-permute-start(bf16[384,384]{1,0:T(8,128)(2,1)S(1)} %fusion.4), channel_id=1, source_target_pairs={{0,32},{32,64},{64,96},{96,0},{1,33},{33,65},{65,97},{97,1},{2,34}... | collective-permute-start | bytes 884744 | tf_op jit(solution)/shard_map/ppermute | solution.py:17
  247.6 8.9 %collective-permute-start.45 = (bf16[384,384]{1,0:T(8,128)(2,1)S(1)}, bf16[384,384]{1,0:T(8,128)(2,1)S(1)}, u32[]{:S(2)}, u32[]{:S(2)}) collective-permute-start(bf16[384,384]{1,0:T(8,128)(2,1)S(1)} %fusion.2), channel_id=1, source_target_pairs={{0,96},{32,0},{64,32},{96,64},{1,97},{33,1},{65,33},{97,65},{2,98}... | collective-permute-start | bytes 884744 | tf_op jit(solution)/shard_map/ppermute | solution.py:17
  260.0 5.2 %collective-permute-start.55 = (f32[8,128]{1,0:T(8,128)S(1)}, f32[8,128]{1,0:T(8,128)S(1)}, u32[]{:S(2)}, u32[]{:S(2)}) collective-permute-start(f32[8,128]{1,0:T(8,128)S(1)} %broadcast_add_fusion), channel_id=1, source_target_pairs={{0,64},{32,96},{64,0},{96,32},{1,65},{33,97},{65,1},{97,33},{2,66}... | collective-permute-start | bytes 12296 | tf_op jit(solution)/shard_map/ppermute | solution.py:17
  269.1 7.8 %collective-permute-start.58 = (f32[8,128]{1,0:T(8,128)S(1)}, f32[8,128]{1,0:T(8,128)S(1)}, u32[]{:S(2)}, u32[]{:S(2)}) collective-permute-start(f32[8,128]{1,0:T(8,128)S(1)} %add_add_fusion.2), channel_id=1, source_target_pairs={{0,16},{8,24},{16,0},{24,8},{1,17},{9,25},{17,1},{25,9},{2,18},{10... | collective-permute-start | bytes 12296 | tf_op jit(solution)/shard_map/ppermute | solution.py:17
  273.8 16.3 %collective-permute-start.46 = (bf16[192,384]{1,0:T(8,128)(2,1)S(1)}, bf16[192,384]{1,0:T(8,128)(2,1)S(1)}, u32[]{:S(2)}, u32[]{:S(2)}) collective-permute-start(bf16[192,384]{1,0:T(8,128)(2,1)S(1)} %get-tuple-element.29), channel_id=1, source_target_pairs={{0,24},{8,0},{16,8},{24,16},{1,25},{9,1},{17,9},{25,17},{2,26},{10... | collective-permute-start | bytes 442376 | tf_op jit(solution)/shard_map/ppermute | solution.py:17
  282.0 6.0 %collective-permute-start.49 = (bf16[96,384]{1,0:T(8,128)(2,1)S(1)}, bf16[96,384]{1,0:T(8,128)(2,1)S(1)}, u32[]{:S(2)}, u32[]{:S(2)}) collective-permute-start(bf16[96,384]{1,0:T(8,128)(2,1)S(1)} %get-tuple-element.31), channel_id=1, source_target_pairs={{0,24},{8,0},{16,8},{24,16},{1,25},{9,1},{17,9},{25,17},{2,26},{10... | collective-permute-start | bytes 221192 | tf_op jit(solution)/shard_map/ppermute | solution.py:17
  283.4 5.8 %collective-permute-start.47 = (bf16[96,384]{1,0:T(8,128)(2,1)S(1)}, bf16[96,384]{1,0:T(8,128)(2,1)S(1)}, u32[]{:S(2)}, u32[]{:S(2)}) collective-permute-start(bf16[96,384]{1,0:T(8,128)(2,1)S(1)} %get-tuple-element.30), channel_id=1, source_target_pairs={{0,8},{8,16},{16,24},{24,0},{1,9},{9,17},{17,25},{25,1},{2,10},{10... | collective-permute-start | bytes 221192 | tf_op jit(solution)/shard_map/ppermute | solution.py:17
  284.1 10.7 %collective-permute-start.51 = (bf16[192,384]{1,0:T(8,128)(2,1)S(1)}, bf16[192,384]{1,0:T(8,128)(2,1)S(1)}, u32[]{:S(2)}, u32[]{:S(2)}) collective-permute-start(bf16[192,384]{1,0:T(8,128)(2,1)S(1)} %get-tuple-element.27), channel_id=1, source_target_pairs={{0,8},{8,16},{16,24},{24,0},{1,9},{9,17},{17,25},{25,1},{2,10},{10... | collective-permute-start | bytes 442376 | tf_op jit(solution)/shard_map/ppermute | solution.py:17
  289.2 5.6 %collective-permute-start.48 = (bf16[96,384]{1,0:T(8,128)(2,1)S(1)}, bf16[96,384]{1,0:T(8,128)(2,1)S(1)}, u32[]{:S(2)}, u32[]{:S(2)}) collective-permute-start(bf16[96,384]{1,0:T(8,128)(2,1)S(1)} %collective-permute-done.47), channel_id=1, source_target_pairs={{0,8},{8,16},{16,24},{24,0},{1,9},{9,17},{17,25},{25,1},{2,10},{10... | collective-permute-start | bytes 221192 | tf_op jit(solution)/shard_map/ppermute | solution.py:17
  (20 other events, 76.9 us)
Sparse Core Ops, SparseCore 0:
  9.6 107.6 all-gather.1
